TPU v7x, 32 devices: a whole 2x2x4 slice. The times are simulated.
32 devices in a mesh: patch: 8 (over z, x), feat: 4 (over y, core).
Axes of the slice: x: 2, y: 2, z: 4, core: 2. Of those that a mesh axis runs over, the one named last changes fastest.
Arguments:
- node_latents: bfloat16 [4096, 512], P('patch'), may hold values from -6 to 6
- edge_latents: bfloat16 [32768, 512], P('patch'), may hold values from -6 to 6
- send_rows: int32 [8, 8, 128], P('patch'), may hold values from 0 to 511, as said below
- edge_slot: int32 [32768], P('patch'), may hold values from 0 to 1023, as said below
- receivers: int32 [32768], P('patch'), may hold values from 0 to 511
- edge_in_w: bfloat16 [3, 3, 512, 512], P(None, None, None, 'feat'), may hold values from -0.15625 to 0.15625
- edge_in_b: float32 [3, 512], P(None, 'feat'), may hold values from -3 to 3
- edge_out_w: bfloat16 [3, 512, 512], P(None, 'feat'), may hold values from -0.25 to 0.25
- edge_gain: float32 [3, 512], replicated, may hold values from 0.5 to 2
- node_in_w: bfloat16 [3, 2, 512, 512], P(None, None, None, 'feat'), may hold values from -0.1875 to 0.1875
- node_in_b: float32 [3, 512], P(None, 'feat'), may hold values from -3 to 3
- node_out_w: bfloat16 [3, 512, 512], P(None, 'feat'), may hold values from -0.25 to 0.25
- node_gain: float32 [3, 512], replicated, may hold values from 0.5 to 2
Outputs:
- node_state: bfloat16 [4096, 512], P('patch')
- edge_state: bfloat16 [32768, 512], P('patch')
Inputs may be any that keep to these rules, and one draw needn't show every extreme that they name: `send_rows`: the rows that one pair (s, d) names at slots used by some edge are distinct; unused slots hold 0. Every edge of patch d names a used slot of some patch s. Each patch names its last node row in the first slot it provides to itself. `edge_slot`: every patch holds exactly 4096 edges, all ending at its own nodes.
All inputs are finite; a program needn't handle non-finite values.
Results may differ from a plain program's by a relative error of at most 0.023.
Values may be sent and summed in bfloat16 or wider, within the bound.
A program may use at most 128 MiB of HBM per device.

v0:
```python
import jax
import jax.numpy as jnp
from jax import lax
from jax.sharding import PartitionSpec as P

LAYERS = 3


def layer_norm(values, scales):
    center = values - jnp.mean(values, axis=-1, keepdims=True)
    spread = jnp.mean(center * center, axis=-1, keepdims=True)
    return center * lax.rsqrt(spread + 1e-05) * scales


def local_split_sum(hidden, weight, pieces):
    share_width = weight.shape[0] // pieces
    running = jnp.zeros((hidden.shape[0], weight.shape[1]), jnp.float32)
    for piece_idx in range(pieces):
        first = piece_idx * share_width
        partial_value = jnp.dot(
            hidden[:, first : first + share_width],
            weight[first : first + share_width],
            preferred_element_type=jnp.float32,
        )
        running = running + partial_value.astype(jnp.bfloat16).astype(jnp.float32)
    return running


def body(
    node_latents,
    edge_latents,
    send_rows,
    edge_slot,
    receivers,
    edge_in_w,
    edge_in_b,
    edge_out_w,
    edge_gain,
    node_in_w,
    node_in_b,
    node_out_w,
    node_gain,
):
    node_rows = node_latents.shape[0]
    edge_rows = edge_latents.shape[0]
    slot_width = send_rows.shape[2]
    out_rows = send_rows[0]
    members = jnp.arange(node_rows, dtype=jnp.int32)
    feat_count = lax.axis_size("feat")
    feat_pos = lax.axis_index("feat")
    node_quarter = node_rows // feat_count
    edge_quarter = edge_rows // feat_count
    remote_rows = lax.all_to_all(out_rows, "patch", split_axis=0, concat_axis=0, tiled=True)
    senders = edge_slot // slot_width * node_rows + remote_rows.reshape(-1)[edge_slot]
    full_edge_in, full_edge_b, full_edge_out, full_node_in, full_node_b, full_node_out = (
        lax.all_gather(edge_in_w, "feat", axis=3, tiled=True),
        lax.all_gather(edge_in_b.astype(jnp.bfloat16), "feat", axis=1, tiled=True).astype(
            edge_in_b.dtype
        ),
        lax.all_gather(edge_out_w, "feat", axis=1, tiled=True),
        lax.all_gather(node_in_w, "feat", axis=3, tiled=True),
        lax.all_gather(node_in_b.astype(jnp.bfloat16), "feat", axis=1, tiled=True).astype(
            node_in_b.dtype
        ),
        lax.all_gather(node_out_w, "feat", axis=1, tiled=True),
    )
    own_receivers = lax.dynamic_slice_in_dim(receivers, feat_pos * edge_quarter, edge_quarter, 0)
    incidence = (members[:, None] == own_receivers[None, :]).astype(jnp.bfloat16)
    edge_state = lax.dynamic_slice_in_dim(edge_latents, feat_pos * edge_quarter, edge_quarter, 0)
    node_state = node_latents
    for layer_idx in range(LAYERS):
        sender_proj = jnp.dot(
            node_state, edge_in_w[layer_idx, 1], preferred_element_type=jnp.float32
        ).astype(jnp.bfloat16)
        every_proj = lax.all_gather(sender_proj, "patch", axis=0, tiled=True)
        fetched = every_proj[senders]
        own_fetched = lax.all_to_all(fetched, "feat", split_axis=0, concat_axis=1, tiled=True)
        receiver_proj = jnp.dot(
            node_state, full_edge_in[layer_idx, 2], preferred_element_type=jnp.float32
        ).astype(jnp.bfloat16)
        preact = jnp.dot(edge_state, full_edge_in[layer_idx, 0], preferred_element_type=jnp.float32)
        preact = (
            preact
            + own_fetched.astype(jnp.float32)
            + receiver_proj[own_receivers].astype(jnp.float32)
            + full_edge_b[layer_idx]
        )
        edge_hidden = jax.nn.silu(preact).astype(jnp.bfloat16)
        edge_total = local_split_sum(edge_hidden, full_edge_out[layer_idx], feat_count)
        message = layer_norm(edge_total, edge_gain[layer_idx])
        update = message.astype(jnp.bfloat16)
        edge_state = (edge_state.astype(jnp.float32) + message).astype(jnp.bfloat16)
        incoming = lax.psum_scatter(
            jnp.dot(incidence, update, preferred_element_type=jnp.float32).astype(jnp.bfloat16),
            "feat",
            scatter_dimension=0,
            tiled=True,
        )
        own_nodes = lax.dynamic_slice_in_dim(node_state, feat_pos * node_quarter, node_quarter, 0)
        node_pre = jnp.dot(
            own_nodes, full_node_in[layer_idx, 0], preferred_element_type=jnp.float32
        )
        node_pre = (
            node_pre
            + jnp.dot(incoming, full_node_in[layer_idx, 1], preferred_element_type=jnp.float32)
            + full_node_b[layer_idx]
        )
        node_hidden = jax.nn.silu(node_pre).astype(jnp.bfloat16)
        node_total = local_split_sum(node_hidden, full_node_out[layer_idx], feat_count)
        node_change = layer_norm(node_total, node_gain[layer_idx])
        own_next = (own_nodes.astype(jnp.float32) + node_change).astype(jnp.bfloat16)
        node_state = lax.all_gather(own_next, "feat", axis=0, tiled=True)
    edge_state = lax.all_gather(edge_state, "feat", axis=0, tiled=True)
    return (node_state, edge_state)


def solution(mesh):
    in_specs = (
        P("patch", None),
        P("patch", None),
        P("patch", None, None),
        P("patch"),
        P("patch"),
        P(None, None, None, "feat"),
        P(None, "feat"),
        P(None, "feat", None),
        P(),
        P(None, None, None, "feat"),
        P(None, "feat"),
        P(None, "feat", None),
        P(),
    )
    out_specs = (P("patch", None), P("patch", None))
    return jax.shard_map(body, mesh=mesh, in_specs=in_specs, out_specs=out_specs, check_vma=False)
```

profile of v0, /device:TPU:10, one launch (start us, length us, event | category | flops | bytes accessed | tf_op | source)
XLA Modules:
  0.0 492.8 jit_solution(7782093489738017242)
XLA Ops:
  7.2 2.0 convolution_convert_fusion.17
  11.3 6.2 %all-to-all-start = ((s32[8,1,128]{2,1,0:T(1,128)}), s32[8,1,128]{2,1,0:T(1,128)S(1)}, u32[]{:S(2)}, u32[]{:S(2)}) async-start(s32[8,1,128]{2,1,0:T(1,128)} %bitcast.3), calls=%async_computation | async-start | bytes 8192 | tf_op jit(solution)/shard_map/all_to_all | solution.py:53
  18.9 5.1 %all_gather.42 = bf16[3,512]{1,0:T(4,128)(2,1)S(1)} all-gather(bf16[3,128]{1,0:T(4,128)(2,1)S(1)} %convert_element_type.290), channel_id=1, replica_groups=mesh['patch'=8,'feat'=4] {'feat'}, dimensions={1}, use_global_device_ids=true | all-gather | bytes 3840 | tf_op jit(solution)/shard_map/all_gather | solution.py:57
  24.0 16.7 %gather_fusion = s32[4096]{0:T(1024)S(1)} fusion(s32[1024]{0:T(1024)S(1)} %bitcast.200, s32[4096]{0:T(1024)S(1)} %fusion.93), kind=kCustom, calls=%fused_computation | custom fusion | bytes 49152 | tf_op jit(solution)/shard_map/gather | solution.py:54
  40.7 9.5 %all-gather.13.cloned.1.call-done = bf16[4096,128]{1,0:T(8,128)(2,1)} async-done(((bf16[512,128]{1,0:T(8,128)(2,1)}), bf16[4096,128]{1,0:T(8,128)(2,1)}) %all-gather.13.cloned.1.call-update) | async-done | bytes 1048592 | tf_op jit(solution)/shard_map/all_gather | solution.py:75
  50.2 15.7 %gather_fusion.1 = bf16[4096,128]{1,0:T(8,128)(2,1)} fusion(bf16[4096,128]{1,0:T(8,128)(2,1)} %all-gather.13.cloned.1.call-done, s32[4096]{0:T(1024)S(1)} %fusion.94), kind=kCustom, calls=%fused_computation.1 | custom fusion | bytes 2113536 | tf_op jit(solution)/shard_map/gather | solution.py:76
  65.9 4.4 all-to-all-start.1
  72.2 29.5 %all-gather.11.cloned.1.call-done = bf16[3,3,512,512]{3,2,1,0:T(8,128)(2,1)} async-done(((bf16[3,3,512,128]{3,2,1,0:T(8,128)(2,1)}), bf16[3,3,512,512]{3,2,1,0:T(8,128)(2,1)}) %all-gather.11.cloned.1.call-update) | async-done | bytes 4718608 | tf_op jit(solution)/shard_map/all_gather | solution.py:56
  101.7 1.5 convolution_convert_fusion.14
  103.2 4.0 gather_fusion.2
  107.2 3.5 multiply_convert_fusion.2
  110.7 12.3 %all-gather.15.cloned.1.call-done = bf16[3,512,512]{2,1,0:T(8,128)(2,1)} async-done(((bf16[3,128,512]{2,1,0:T(8,128)(2,1)}), bf16[3,512,512]{2,1,0:T(8,128)(2,1)}) %all-gather.15.cloned.1.call-update) | async-done | bytes 1572880 | tf_op jit(solution)/shard_map/all_gather | solution.py:60
  123.0 1.5 convolution_convert_fusion.10
  124.4 1.5 convolution_convert_fusion.11
  125.9 1.5 convolution_convert_fusion.9
  127.4 1.6 fusion.104
  130.0 1.6 fusion.12
  132.3 5.1 %all_gather.44 = bf16[3,512]{1,0:T(4,128)(2,1)S(1)} all-gather(bf16[3,128]{1,0:T(4,128)(2,1)S(1)} %convert_element_type.303), channel_id=1, replica_groups=mesh['patch'=8,'feat'=4] {'feat'}, dimensions={1}, use_global_device_ids=true | all-gather | bytes 3840 | tf_op jit(solution)/shard_map/all_gather | solution.py:62
  138.6 14.8 %all-gather.9.cloned.1.call-done = bf16[3,2,512,512]{3,2,1,0:T(8,128)(2,1)} async-done(((bf16[3,2,512,128]{3,2,1,0:T(8,128)(2,1)}), bf16[3,2,512,512]{3,2,1,0:T(8,128)(2,1)}) %all-gather.9.cloned.1.call-update) | async-done | bytes 3145744 | tf_op jit(solution)/shard_map/all_gather | solution.py:61
  153.4 1.3 fusion.56
  154.7 23.2 %reduce-scatter.4.cloned.1.call-done = bf16[128,512]{1,0:T(8,128)(2,1)} async-done(((bf16[512,512]{1,0:T(8,128)(2,1)}), bf16[128,512]{1,0:T(8,128)(2,1)}) %reduce-scatter.4.cloned.1.call-update) | async-done | bytes 131088 | tf_op jit(solution)/shard_map/reduce_scatter | solution.py:93
  178.0 1.3 multiply_convert_fusion.5
  179.3 19.8 %all-gather.17.cloned.1.call-done = bf16[3,512,512]{2,1,0:T(8,128)(2,1)} async-done(((bf16[3,128,512]{2,1,0:T(8,128)(2,1)}), bf16[3,512,512]{2,1,0:T(8,128)(2,1)}) %all-gather.17.cloned.1.call-update) | async-done | bytes 1572880 | tf_op jit(solution)/shard_map/all_gather | solution.py:65
  204.8 7.2 %all_gather.46 = bf16[512,512]{1,0:T(8,128)(2,1)S(1)} all-gather(bf16[128,512]{1,0:T(8,128)(2,1)S(1)} %add_convert_fusion.5), channel_id=1, replica_groups=mesh['patch'=8,'feat'=4] {'feat'}, dimensions={0}, use_global_device_ids=true | all-gather | bytes 655360 | tf_op jit(solution)/shard_map/all_gather | solution.py:112
  212.8 1.9 convolution_convert_fusion.16
  214.7 38.5 %all-gather.19.cloned.1.call-done = bf16[4096,128]{1,0:T(8,128)(2,1)} async-done(((bf16[512,128]{1,0:T(8,128)(2,1)}), bf16[4096,128]{1,0:T(8,128)(2,1)}) %all-gather.19.cloned.1.call-update) | async-done | bytes 1048592 | tf_op jit(solution)/shard_map/all_gather | solution.py:75
  253.2 15.7 %gather_fusion.3 = bf16[4096,128]{1,0:T(8,128)(2,1)} fusion(bf16[4096,128]{1,0:T(8,128)(2,1)} %all-gather.19.cloned.1.call-done, s32[4096]{0:T(1024)S(1)} %fusion.94), kind=kCustom, calls=%fused_computation.3 | custom fusion | bytes 2113536 | tf_op jit(solution)/shard_map/gather | solution.py:76
  268.9 4.3 all-to-all-start.2
  273.4 1.3 copy.30
  274.8 2.7 add_convert_fusion.2
  277.4 1.5 convolution_convert_fusion.13
  278.9 4.0 gather_fusion.4
  282.9 4.8 all-to-all-done.2
  287.7 2.6 multiply_convert_fusion.1
  290.3 1.4 convolution_convert_fusion.6
  291.7 1.4 convolution_convert_fusion.7
  293.1 1.4 convolution_convert_fusion.5
  294.5 1.6 fusion.106
  296.7 1.6 fusion.13
  298.4 1.3 fusion.55
  299.8 20.1 %reduce-scatter.6.cloned.1.call-done = bf16[128,512]{1,0:T(8,128)(2,1)} async-done(((bf16[512,512]{1,0:T(8,128)(2,1)}), bf16[128,512]{1,0:T(8,128)(2,1)}) %reduce-scatter.6.cloned.1.call-update) | async-done | bytes 131088 | tf_op jit(solution)/shard_map/reduce_scatter | solution.py:93
  319.9 1.4 multiply_convert_fusion.4
  327.0 6.8 %all_gather.48 = bf16[512,512]{1,0:T(8,128)(2,1)S(1)} all-gather(bf16[128,512]{1,0:T(8,128)(2,1)S(1)} %add_convert_fusion.4), channel_id=1, replica_groups=mesh['patch'=8,'feat'=4] {'feat'}, dimensions={0}, use_global_device_ids=true | all-gather | bytes 655360 | tf_op jit(solution)/shard_map/all_gather | solution.py:112
  334.6 1.9 convolution_convert_fusion.15
  336.5 38.8 %all-gather.21.cloned.1.call-done = bf16[4096,128]{1,0:T(8,128)(2,1)} async-done(((bf16[512,128]{1,0:T(8,128)(2,1)}), bf16[4096,128]{1,0:T(8,128)(2,1)}) %all-gather.21.cloned.1.call-update) | async-done | bytes 1048592 | tf_op jit(solution)/shard_map/all_gather | solution.py:75
  375.3 15.7 %gather_fusion.5 = bf16[4096,128]{1,0:T(8,128)(2,1)} fusion(bf16[4096,128]{1,0:T(8,128)(2,1)} %all-gather.21.cloned.1.call-done, s32[4096]{0:T(1024)S(1)} %fusion.94), kind=kCustom, calls=%fused_computation.5 | custom fusion | bytes 2113536 | tf_op jit(solution)/shard_map/gather | solution.py:76
  391.0 4.3 all-to-all-start.3
  395.3 1.4 add_convert_fusion.1
  396.7 1.5 convolution_convert_fusion.12
  398.2 4.0 gather_fusion.6
  402.2 7.6 %all-to-all-done.3 = bf16[4,1024,128]{2,1,0:T(8,128)(2,1)} async-done(((bf16[4,1024,128]{2,1,0:T(8,128)(2,1)}), bf16[4,1024,128]{2,1,0:T(8,128)(2,1)}, u32[]{:S(2)}, u32[]{:S(2)}) %all-to-all-start.3) | async-done | bytes 1048608 | tf_op jit(solution)/shard_map/all_to_all | solution.py:77
  409.8 2.6 multiply_convert_fusion
  412.4 1.4 convolution_convert_fusion.2
  413.8 1.4 convolution_convert_fusion.3
  415.2 1.4 convolution_convert_fusion.1
  416.5 1.6 fusion.108
  418.8 1.6 fusion.14
  420.5 1.4 add_convert_fusion
  421.9 1.3 fusion.54
  423.3 18.7 %reduce-scatter.8.cloned.1.call-done = bf16[128,512]{1,0:T(8,128)(2,1)} async-done(((bf16[512,512]{1,0:T(8,128)(2,1)}), bf16[128,512]{1,0:T(8,128)(2,1)}) %reduce-scatter.8.cloned.1.call-update) | async-done | bytes 131088 | tf_op jit(solution)/shard_map/reduce_scatter | solution.py:93
  442.0 1.4 multiply_convert_fusion.3
  449.0 7.4 %all_gather.50 = bf16[512,512]{1,0:T(8,128)(2,1)S(1)} all-gather(bf16[128,512]{1,0:T(8,128)(2,1)S(1)} %add_convert_fusion.3), channel_id=1, replica_groups=mesh['patch'=8,'feat'=4] {'feat'}, dimensions={0}, use_global_device_ids=true | all-gather | bytes 655360 | tf_op jit(solution)/shard_map/all_gather | solution.py:112
  456.4 22.6 %all-gather.23.cloned.1.call-done = bf16[4096,512]{0,1:T(8,128)(2,1)} async-done(((bf16[1024,512]{0,1:T(8,128)(2,1)}), bf16[4096,512]{0,1:T(8,128)(2,1)}) %all-gather.23.cloned.1.call-update) | async-done | bytes 4194320 | tf_op jit(solution)/shard_map/all_gather | solution.py:113
  479.0 6.4 %copy.29 = bf16[4096,512]{1,0:T(8,128)(2,1)} copy(bf16[4096,512]{0,1:T(8,128)(2,1)} %all-gather.23.cloned.1.call-done) | data formatting | bytes 8388608
  (130 shorter events, 29.1 us)
Async XLA Ops:
  7.2 10.4 %copy-start.9 = (s32[4096]{0:T(1024)S(1)}, s32[4096]{0:T(1024)}, u32[]{:S(2)}) copy-start(s32[4096]{0:T(1024)} %param.16) | copy-start | bytes 49156
  7.2 43.0 %all-gather.13.cloned.1.call-start = ((), (), s32[]{:S(2)}) async-start(), calls=%async_computation.9 | async-start | bytes 1179648 | tf_op jit(solution)/shard_map/all_gather | solution.py:75
  9.3 9.6 %copy-start.25 = (f32[3,128]{1,0:T(4,128)S(1)}, f32[3,128]{1,0:T(4,128)}, u32[]{:S(2)}) copy-start(f32[3,128]{1,0:T(4,128)} %param.19) | copy-start | bytes 4612
  9.3 92.4 %all-gather.11.cloned.1.call-start = ((), (), s32[]{:S(2)}) async-start(), calls=%async_computation.8 | async-start | bytes 5898240 | tf_op jit(solution)/shard_map/all_gather | solution.py:56
  10.0 112.9 %all-gather.15.cloned.1.call-start = ((), (), s32[]{:S(2)}) async-start(), calls=%async_computation.10 | async-start | bytes 1966080 | tf_op jit(solution)/shard_map/all_gather | solution.py:60
  10.8 142.6 %all-gather.9.cloned.1.call-start = ((), (), s32[]{:S(2)}) async-start(), calls=%async_computation.7 | async-start | bytes 3932160 | tf_op jit(solution)/shard_map/all_gather | solution.py:61
  11.3 12.6 %all-to-all-start = ((s32[8,1,128]{2,1,0:T(1,128)}), s32[8,1,128]{2,1,0:T(1,128)S(1)}, u32[]{:S(2)}, u32[]{:S(2)}) async-start(s32[8,1,128]{2,1,0:T(1,128)} %bitcast.3), calls=%async_computation | async-start | bytes 8192 | tf_op jit(solution)/shard_map/all_to_all | solution.py:53
  65.9 5.7 %copy-start.21 = (f32[3,512]{1,0:T(4,128)S(1)}, f32[3,512]{1,0:T(4,128)}, u32[]{:S(2)}) copy-start(f32[3,512]{1,0:T(4,128)} %param.21) | copy-start | bytes 18436
  65.9 35.8 %copy-start.6 = (bf16[512,512]{1,0:T(8,128)(2,1)S(1)}, bf16[512,512]{1,0:T(8,128)(2,1)}, u32[]{:S(2)}) copy-start(bf16[512,512]{1,0:T(8,128)(2,1)} %param.13) | copy-start | bytes 1572868
  65.9 41.3 %all-to-all-start.1 = ((bf16[4,1024,128]{2,1,0:T(8,128)(2,1)}), bf16[4,1024,128]{2,1,0:T(8,128)(2,1)}, u32[]{:S(2)}, u32[]{:S(2)}) async-start(bf16[4,1024,128]{2,1,0:T(8,128)(2,1)} %bitcast.5), calls=%async_computation.1 | async-start | bytes 2097152 | tf_op jit(solution)/shard_map/all_to_all | solution.py:77
  70.3 107.7 %reduce-scatter.4.cloned.1.call-start = ((), (), s32[]{:S(2)}) async-start(), calls=%async_computation.11 | async-start | bytes 655360 | tf_op jit(solution)/shard_map/reduce_scatter | solution.py:93
  71.0 36.1 %copy-start.7 = (s32[1024]{0:T(1024)}, s32[1024]{0:T(1024)S(1)}, u32[]{:S(2)}) copy-start(s32[1024]{0:T(1024)S(1)} %get-tuple-element.8) | copy-start | bytes 12292
  71.0 58.3 %copy-start.23 = (s32[1024]{0:T(1024)}, s32[1024]{0:T(1024)S(1)}, u32[]{:S(2)}) copy-start(s32[1024]{0:T(1024)S(1)} %get-tuple-element.9) | copy-start | bytes 12292
  72.2 57.2 %copy-start.17 = (f32[1,512]{1,0:T(1,128)}, f32[1,512]{1,0:T(1,128)S(1)}, u32[]{:S(2)}) copy-start(f32[1,512]{1,0:T(1,128)S(1)} %get-tuple-element.14) | copy-start | bytes 6148
  129.1 0.6 copy-start.10
  129.4 0.6 copy-start.12
  130.0 2.3 copy-start.26
  130.0 8.0 %copy-start.22 = (f32[3,512]{1,0:T(4,128)S(1)}, f32[3,512]{1,0:T(4,128)}, u32[]{:S(2)}) copy-start(f32[3,512]{1,0:T(4,128)} %param.25) | copy-start | bytes 18436
  131.6 67.5 %all-gather.17.cloned.1.call-start = ((), (), s32[]{:S(2)}) async-start(), calls=%async_computation.12 | async-start | bytes 1966080 | tf_op jit(solution)/shard_map/all_gather | solution.py:65
  132.2 121.0 %all-gather.19.cloned.1.call-start = ((), (), s32[]{:S(2)}) async-start(), calls=%async_computation.13 | async-start | bytes 1179648 | tf_op jit(solution)/shard_map/all_gather | solution.py:75
  179.3 24.5 %copy-start.20 = (f32[1,512]{1,0:T(1,128)S(1)}, f32[1,512]{1,0:T(1,128)}, u32[]{:S(2)}) copy-start(f32[1,512]{1,0:T(1,128)} %get-tuple-element.11) | copy-start | bytes 6148
  212.0 0.8 copy-start.4
  268.9 5.8 %copy-start.11 = (f32[1024]{0:T(1024)S(1)}, f32[1024]{0:T(1024)}, u32[]{:S(2)}) copy-start(f32[1024]{0:T(1024)} %copy-done.10) | copy-start | bytes 12292
  268.9 5.8 %copy-start.13 = (f32[1024]{0:T(1024)S(1)}, f32[1024]{0:T(1024)}, u32[]{:S(2)}) copy-start(f32[1024]{0:T(1024)} %copy-done.12) | copy-start | bytes 12292
  268.9 5.8 %copy-start.18 = (f32[1,512]{1,0:T(1,128)S(1)}, f32[1,512]{1,0:T(1,128)}, u32[]{:S(2)}) copy-start(f32[1,512]{1,0:T(1,128)} %copy-done.17) | copy-start | bytes 6148
  268.9 18.8 %all-to-all-start.2 = ((bf16[4,1024,128]{2,1,0:T(8,128)(2,1)}), bf16[4,1024,128]{2,1,0:T(8,128)(2,1)}, u32[]{:S(2)}, u32[]{:S(2)}) async-start(bf16[4,1024,128]{2,1,0:T(8,128)(2,1)} %bitcast.24), calls=%async_computation.3 | async-start | bytes 2097152 | tf_op jit(solution)/shard_map/all_to_all | solution.py:77
  273.2 46.7 %reduce-scatter.6.cloned.1.call-start = ((), (), s32[]{:S(2)}) async-start(), calls=%async_computation.14 | async-start | bytes 655360 | tf_op jit(solution)/shard_map/reduce_scatter | solution.py:93
  274.7 2.7 copy-start.5
  274.7 4.2 copy-start.8
  278.9 8.8 %copy-start = (bf16[1024,512]{0,1:T(8,128)(2,1)S(1)}, bf16[1024,512]{0,1:T(8,128)(2,1)}, u32[]{:S(2)}) copy-start(bf16[1024,512]{0,1:T(8,128)(2,1)} %add_convert_fusion.2) | copy-start | bytes 3145732
  278.9 8.8 %copy-start.29 = (f32[1,512]{1,0:T(1,128)S(1)}, f32[1,512]{1,0:T(1,128)}, u32[]{:S(2)}) copy-start(f32[1,512]{1,0:T(1,128)} %get-tuple-element.20) | copy-start | bytes 6148
  296.0 0.7 copy-start.16
  296.0 0.7 copy-start.24
  296.7 23.2 %copy-start.30 = (f32[1,512]{1,0:T(1,128)S(1)}, f32[1,512]{1,0:T(1,128)}, u32[]{:S(2)}) copy-start(f32[1,512]{1,0:T(1,128)} %get-tuple-element.17) | copy-start | bytes 6148
  298.4 76.9 %all-gather.21.cloned.1.call-start = ((), (), s32[]{:S(2)}) async-start(), calls=%async_computation.15 | async-start | bytes 1179648 | tf_op jit(solution)/shard_map/all_gather | solution.py:75
  319.9 6.0 %copy-start.19 = (f32[1,512]{1,0:T(1,128)S(1)}, f32[1,512]{1,0:T(1,128)}, u32[]{:S(2)}) copy-start(f32[1,512]{1,0:T(1,128)} %get-tuple-element.12) | copy-start | bytes 6148
  333.8 0.8 copy-start.2
  391.0 18.8 %all-to-all-start.3 = ((bf16[4,1024,128]{2,1,0:T(8,128)(2,1)}), bf16[4,1024,128]{2,1,0:T(8,128)(2,1)}, u32[]{:S(2)}, u32[]{:S(2)}) async-start(bf16[4,1024,128]{2,1,0:T(8,128)(2,1)} %bitcast.43), calls=%async_computation.5 | async-start | bytes 2097152 | tf_op jit(solution)/shard_map/all_to_all | solution.py:77
  395.2 46.7 %reduce-scatter.8.cloned.1.call-start = ((), (), s32[]{:S(2)}) async-start(), calls=%async_computation.16 | async-start | bytes 655360 | tf_op jit(solution)/shard_map/reduce_scatter | solution.py:93
  395.3 1.4 copy-start.3
  398.2 11.6 %copy-start.1 = (bf16[1024,512]{0,1:T(8,128)(2,1)S(1)}, bf16[1024,512]{0,1:T(8,128)(2,1)}, u32[]{:S(2)}) copy-start(bf16[1024,512]{0,1:T(8,128)(2,1)} %add_convert_fusion.1) | copy-start | bytes 3145732
  398.2 11.6 %copy-start.27 = (f32[1,512]{1,0:T(1,128)S(1)}, f32[1,512]{1,0:T(1,128)}, u32[]{:S(2)}) copy-start(f32[1,512]{1,0:T(1,128)} %get-tuple-element.19) | copy-start | bytes 6148
  418.1 0.7 copy-start.14
  420.4 21.5 %copy-start.28 = (f32[1,512]{1,0:T(1,128)S(1)}, f32[1,512]{1,0:T(1,128)}, u32[]{:S(2)}) copy-start(f32[1,512]{1,0:T(1,128)} %get-tuple-element.16) | copy-start | bytes 6148
  420.4 58.6 %all-gather.23.cloned.1.call-start = ((), (), s32[]{:S(2)}) async-start(), calls=%async_computation.17 | async-start | bytes 5242880 | tf_op jit(solution)/shard_map/all_gather | solution.py:113
  442.0 6.0 %copy-start.15 = (f32[1,512]{1,0:T(1,128)S(1)}, f32[1,512]{1,0:T(1,128)}, u32[]{:S(2)}) copy-start(f32[1,512]{1,0:T(1,128)} %get-tuple-element.10) | copy-start | bytes 6148
Sparse Core Ops, SparseCore 0:
  10.7 39.4 all-gather.12
  51.7 49.9 all-gather.10
  103.3 19.6 all-gather.14
  124.4 28.9 all-gather.8
  156.3 21.6 reduce-scatter.3
  179.4 19.6 all-gather.16
  214.8 38.3 all-gather.18
  298.5 21.3 reduce-scatter.5
  336.6 38.6 all-gather.20
  420.6 21.3 reduce-scatter.7
  444.2 34.8 all-gather.22
where the time goes:
time: 496 us; the launch traced here: 493 us
  waiting for transfers between devices  263 us (53%)
  local copies, waits for them, and re-layouts  90.9 us (18%)
  matrix products  62.5 us (13%)
  blocking collectives  31.5 us (6%)
  starting transfers between devices  19.7 us (4%)
  between operations  14.5 us (3%)
  other arithmetic  10.8 us (2%)
    all_gather x3, waiting for transfers between devices, body(): every_proj = lax.all_gather(sender_proj, 'patch', axis=0, tiled=True)  86.8 us
    reduce_scatter x3, waiting for transfers between devices, body(): lax.psum_scatter(jnp.dot(incidence, update, preferred_element_type=jnp.fl...  62.1 us
    gather x3, local copies, waits for them, and re-layouts, body(): fetched = every_proj[senders]  47.1 us
    dot_general x24, matrix products, local_split_sum(): jnp.dot(hidden[:, first:first + share_width], weight[first:first + share_...  30.6 us
    all_gather x1, waiting for transfers between devices, body(): lax.all_gather(edge_in_w, 'feat', axis=3, tiled=True)  29.5 us
    all_gather x1, waiting for transfers between devices, body(): edge_state = lax.all_gather(edge_state, 'feat', axis=0, tiled=True)  22.6 us
    all_gather x3, blocking collectives, body(): node_state = lax.all_gather(own_next, 'feat', axis=0, tiled=True)  21.3 us
    all_gather x1, waiting for transfers between devices, body(): lax.all_gather(node_out_w, 'feat', axis=1, tiled=True)  19.8 us
  transfers between devices with their start and end apart: 15, of which 13 were waited for; matrix products, arithmetic and copies ran while one was open for 17% of the time, Pallas kernels for 0%

commit v1 on v0

v1 whole, which is shorter than its diff:
```python
import functools

import jax
import jax.numpy as jnp
from jax import lax
from jax.experimental import pallas as pl
from jax.experimental.pallas import tpu as pltpu
from jax.sharding import PartitionSpec as P

BF = jnp.bfloat16
F32 = jnp.float32
MESH = pl.DeviceIdType.MESH
BLOCK = 256
LANES = 128


def silu(v):
    return v * (0.5 + 0.5 * jnp.tanh(0.5 * v))


def norm(v, gain):
    center = v - jnp.mean(v, axis=-1, keepdims=True)
    spread = jnp.mean(center * center, axis=-1, keepdims=True)
    return center * lax.rsqrt(spread + 1e-05) * gain


def dot(a, b):
    return jnp.dot(a, b, preferred_element_type=F32)


def kernel(
    patches,
    feats,
    nodes_in,
    edges_in,
    send_rows,
    slots,
    recvs,
    ein,
    eb,
    eo,
    egain,
    nin,
    nb,
    no,
    ngain,
    nodes_out,
    edges_out,
    own_b,
    all_b,
    w_send,
    w_edge,
    w_eo,
    w_nin,
    w_no,
    table,
    hot_slot,
    hot_recv,
    hot_recv_t,
    hot_send,
    edge,
    pre,
    upd,
    node,
    proj,
    picked,
    part,
    other,
    rproj,
    sem_in,
    sem_loc,
    sem_ys,
    sem_yr,
    sem_cs,
    sem_cr,
    sem_bs,
    sem_br,
    sem_ts,
    sem_tr,
    sem_fs,
    sem_fr,
    sem_ps,
    sem_pr,
    sem_os,
    sem_or,
    sem_ol,
):
    layers = ein.shape[0]
    me = lax.axis_index("patch")
    f = lax.axis_index("feat")
    core = lax.rem(f, 2)
    mate = f + 1 - 2 * core
    half_feats = feats // 2
    width = ein.shape[3]
    half_width = half_feats * width
    cap = send_rows.shape[1]
    half = edge.shape[0]
    nrows = node.shape[0]
    blocks = half // BLOCK

    def place(q):
        return lax.rem(q, 2) * half_feats + q // 2

    def cols(q):
        return pl.ds(pl.multiple_of(place(q) * width, width), width)

    def source(k):
        l, i = divmod(k, 6)
        return (ein.at[l, 1], ein.at[l, 0], ein.at[l, 2], eo.at[l], nin.at[l], no.at[l])[i]

    def target(k, q):
        l, i = divmod(k, 6)
        if i == 0:
            return w_send.at[l, :, pl.ds(pl.multiple_of(q // 2 * width, width), width)]
        if i in (1, 2):
            return w_edge.at[l, i - 1, :, cols(q)]
        if i == 3:
            return w_eo.at[l, cols(q), :]
        if i == 4:
            return w_nin.at[l, :, :, cols(q)]
        return w_no.at[l, cols(q), :]

    def remote(src, dst, ss, rs, **where):
        return pltpu.make_async_remote_copy(
            src_ref=src, dst_ref=dst, send_sem=ss, recv_sem=rs, device_id=where, device_id_type=MESH
        )

    def local_copy(k):
        return pltpu.make_async_copy(source(k), target(k, f), sem_loc.at[k])

    def across(k, j, q):
        return remote(
            source(k), target(k, q), sem_ys.at[k, j], sem_yr.at[k, j],
            feat=lax.rem(f + 2 * j, feats),
        )

    def beside(k, j, q):
        src = source(k) if j == 0 else target(k, q)
        return remote(src, target(k, q), sem_cs.at[k, j], sem_cr.at[k, j], feat=mate)

    def back(q, j):
        return lax.rem(q + feats - 2 * j, feats)

    def start_weights(l):
        for k in range(6 * l, 6 * l + 6):
            for j in range(1, half_feats):
                across(k, j, f).start()
            local_copy(k).start()
            if k % 6:
                beside(k, 0, f).start()

    def advance(k):
        for j in range(1, half_feats):
            across(k, j, back(f, j)).wait_recv()
            if k % 6:
                beside(k, j, back(f, j)).start()

    def acquire(k):
        local_copy(k).wait()
        if k % 6:
            for j in range(half_feats):
                beside(k, j, back(mate, j)).wait_recv()

    def bias_copy(j, q):
        return remote(
            own_b, all_b.at[q], sem_bs.at[j], sem_br.at[j], feat=lax.rem(f + j, feats)
        )

    barrier = pltpu.get_barrier_semaphore()
    for j in range(1, feats):
        pl.semaphore_signal(
            barrier, inc=1, device_id={"feat": lax.rem(f + j, feats)}, device_id_type=MESH
        )

    def greet(j, carry):
        pl.semaphore_signal(
            barrier, inc=1, device_id={"patch": lax.rem(me + j, patches)}, device_id_type=MESH
        )
        return carry

    lax.fori_loop(1, patches, greet, 0)
    load_nodes = pltpu.make_async_copy(nodes_in, node, sem_in.at[0])
    load_edges = pltpu.make_async_copy(
        edges_in.at[pl.ds(pl.multiple_of(core * half, half), half)], edge, sem_in.at[1]
    )
    load_nodes.start()
    load_edges.start()
    own_b[...] = jnp.zeros_like(own_b)
    own_b[0:layers] = eb[...]
    own_b[layers : 2 * layers] = nb[...]
    all_b[f] = own_b[...]
    pl.semaphore_wait(barrier, feats - 1 + patches - 1)
    for j in range(1, feats):
        bias_copy(j, f).start()
    start_weights(0)

    lines = half // LANES
    first_line = core * lines

    def column(row):
        return jnp.transpose(jnp.broadcast_to(row, (LANES, LANES)))

    def spread_hot(ref, row0, col):
        for c in range(ref.shape[1] // LANES):
            ids = lax.broadcasted_iota(jnp.int32, (LANES, LANES), 1) + c * LANES
            ref[pl.ds(row0, LANES), c * LANES : (c + 1) * LANES] = jnp.where(
                ids == col, 1.0, 0.0
            ).astype(BF)

    def build_send(i, carry):
        spread_hot(hot_send, pl.multiple_of(i * LANES, LANES), column(send_rows[pl.ds(i, 1), :]))
        return carry

    lax.fori_loop(0, patches, build_send, 0)

    def build_edge(i, carry):
        at = pl.multiple_of(i * LANES, LANES)
        row = recvs[pl.ds(first_line + i, 1), :]
        ids = lax.broadcasted_iota(jnp.int32, (nrows, LANES), 0)
        hot_recv_t[:, pl.ds(at, LANES)] = jnp.where(ids == row, 1.0, 0.0).astype(BF)
        spread_hot(hot_recv, at, column(row))
        spread_hot(hot_slot, at, column(slots[pl.ds(first_line + i, 1), :]))
        return carry

    def table_copy(l, s, d):
        return remote(
            picked.at[pl.ds(pl.multiple_of(d * cap, cap), cap)],
            table.at[
                l,
                pl.ds(pl.multiple_of(s * cap, cap), cap),
                pl.ds(pl.multiple_of(core * half_width, half_width), half_width),
            ],
            sem_ts.at[l, d],
            sem_tr.at[l, s],
            patch=d,
        )

    def table_pass(l, s, c):
        part_of = table.at[
            l,
            pl.ds(pl.multiple_of(s * cap, cap), cap),
            pl.ds(pl.multiple_of(c * half_width, half_width), half_width),
        ]
        return remote(part_of, part_of, sem_fs.at[l, s], sem_fr.at[l, s], feat=mate)

    def bias(row):
        order = sorted(range(feats), key=lambda q: (q % 2) * half_feats + q // 2)
        return jnp.concatenate([all_b[q, row : row + 1, :] for q in order], axis=1)

    def out_local(b):
        rows = pl.ds(pl.multiple_of(b * BLOCK, BLOCK), BLOCK)
        dst = pl.ds(pl.multiple_of(core * half + b * BLOCK, BLOCK), BLOCK)
        return pltpu.make_async_copy(edge.at[rows], edges_out.at[dst], sem_ol.at[b])

    def out_remote(b, c):
        rows = pl.ds(pl.multiple_of(b * BLOCK, BLOCK), BLOCK)
        dst = pl.ds(pl.multiple_of(c * half + b * BLOCK, BLOCK), BLOCK)
        return remote(edge.at[rows], edges_out.at[dst], sem_os.at[b], sem_or.at[b], feat=mate)

    load_nodes.wait()
    for l in range(layers):
        k0 = 6 * l
        advance(k0)
        acquire(k0)
        proj[...] = dot(node[...], w_send[l]).astype(BF)

        def pick(j, carry, l=l):
            d = lax.rem(me + j, patches)
            rows = pl.ds(pl.multiple_of(d * cap, cap), cap)
            picked[rows, :] = dot(hot_send[rows, :], proj[...]).astype(BF)
            table_copy(l, me, d).start()
            return carry

        lax.fori_loop(1, patches, pick, 0)
        mine = pl.ds(pl.multiple_of(me * cap, cap), cap)
        table[
            l, mine, pl.ds(pl.multiple_of(core * half_width, half_width), half_width)
        ] = dot(hot_send[mine, :], proj[...]).astype(BF)
        table_pass(l, me, core).start()
        if l == 0:
            lax.fori_loop(0, lines, build_edge, 0)
            load_edges.wait()
            for j in range(1, feats):
                bias_copy(j, lax.rem(f + feats - j, feats)).wait_recv()
        advance(k0 + 1)
        advance(k0 + 2)
        acquire(k0 + 1)
        acquire(k0 + 2)
        for b in range(nrows // BLOCK):
            rows = slice(b * BLOCK, (b + 1) * BLOCK)
            rproj[rows] = dot(node[rows], w_edge[l, 1]).astype(BF)
        eb_row = bias(l)

        def begin(b, carry, l=l, eb_row=eb_row):
            rows = pl.ds(pl.multiple_of(b * BLOCK, BLOCK), BLOCK)
            pre[rows, :] = (
                dot(edge[rows, :], w_edge[l, 0]) + dot(hot_recv[rows, :], rproj[...]) + eb_row
            )
            return carry

        lax.fori_loop(0, blocks, begin, 0)

        def relay(j, carry, l=l):
            s = lax.rem(me + j, patches)
            table_copy(l, s, me).wait_recv()
            table_pass(l, s, core).start()
            return carry

        lax.fori_loop(1, patches, relay, 0)
        advance(k0 + 3)

        def settle(s, carry, l=l):
            table_pass(l, s, 1 - core).wait_recv()
            return carry

        lax.fori_loop(0, patches, settle, 0)
        acquire(k0 + 3)
        if l + 1 < layers:
            start_weights(l + 1)

        def work(b, carry, l=l):
            rows = pl.ds(pl.multiple_of(b * BLOCK, BLOCK), BLOCK)
            hidden = silu(pre[rows, :] + dot(hot_slot[rows, :], table[l])).astype(BF)
            message = norm(dot(hidden, w_eo[l]), egain[l : l + 1, :])
            upd[rows, :] = message.astype(BF)
            edge[rows, :] = (edge[rows, :].astype(F32) + message).astype(BF)
            if l == layers - 1:
                out_local(b).start()
                out_remote(b, core).start()
            return carry

        lax.fori_loop(0, blocks, work, 0)
        for b in range(nrows // BLOCK):
            rows = slice(b * BLOCK, (b + 1) * BLOCK)
            part[rows] = dot(hot_recv_t[rows, :], upd[...]).astype(BF)
        swap = remote(part, other.at[l], sem_ps.at[l], sem_pr.at[l], feat=mate)
        swap.start()
        advance(k0 + 4)
        advance(k0 + 5)
        acquire(k0 + 4)
        acquire(k0 + 5)
        swap.wait()
        nb_row = bias(layers + l)
        for b in range(nrows // BLOCK):
            rows = slice(b * BLOCK, (b + 1) * BLOCK)
            incoming = (part[rows].astype(F32) + other[l, rows].astype(F32)).astype(BF)
            hidden = silu(
                dot(node[rows], w_nin[l, 0]) + dot(incoming, w_nin[l, 1]) + nb_row
            ).astype(BF)
            change = norm(dot(hidden, w_no[l]), ngain[l : l + 1, :])
            node[rows] = (node[rows].astype(F32) + change).astype(BF)

        def drain(j, carry, l=l):
            table_copy(l, me, lax.rem(me + j, patches)).wait_send()
            return carry

        lax.fori_loop(1, patches, drain, 0)

    store_nodes = pltpu.make_async_copy(node, nodes_out, sem_in.at[2])
    store_nodes.start()
    for j in range(1, feats):
        bias_copy(j, f).wait_send()
    for k in range(6 * layers):
        for j in range(1, half_feats):
            across(k, j, f).wait_send()
        if k % 6:
            for j in range(half_feats):
                beside(k, j, back(f, j)).wait_send()
    for l in range(layers):

        def done(s, carry, l=l):
            table_pass(l, s, core).wait_send()
            return carry

        lax.fori_loop(0, patches, done, 0)

    def finish(b, carry):
        out_local(b).wait()
        out_remote(b, core).wait_send()
        out_remote(b, 1 - core).wait_recv()
        return carry

    lax.fori_loop(0, blocks, finish, 0)
    store_nodes.wait()


def body(patches, feats, *args):
    (nodes, edges, send_rows, edge_slot, receivers, ein, eb, eo, egain, nin, nb, no, ngain) = args
    layers = ein.shape[0]
    nrows, dim = nodes.shape
    erows = edges.shape[0]
    half = erows // 2
    width = ein.shape[3]
    hid = width * feats
    cap = send_rows.shape[2]
    slots = patches * cap
    blocks = half // BLOCK
    vmem = pltpu.VMEM
    bias_rows = -(-2 * layers // 8) * 8
    dma = pltpu.SemaphoreType.DMA
    any_spec = pl.BlockSpec(memory_space=pl.ANY)
    v_spec = pl.BlockSpec(memory_space=vmem)
    call = pl.pallas_call(
        functools.partial(kernel, patches, feats),
        out_shape=(
            jax.ShapeDtypeStruct((nrows, dim), BF),
            jax.ShapeDtypeStruct((erows, dim), BF),
        ),
        in_specs=[
            any_spec, any_spec, v_spec, v_spec, v_spec, any_spec, v_spec, any_spec, v_spec,
            any_spec, v_spec, any_spec, v_spec,
        ],
        out_specs=(any_spec, any_spec),
        scratch_shapes=[
            vmem((bias_rows, width), F32),
            vmem((feats, bias_rows, width), F32),
            vmem((layers, dim, hid // 2), BF),
            vmem((layers, 2, dim, hid), BF),
            vmem((layers, hid, dim), BF),
            vmem((layers, 2, dim, hid), BF),
            vmem((layers, hid, dim), BF),
            vmem((layers, slots, hid), BF),
            vmem((half, slots), BF),
            vmem((half, nrows), BF),
            vmem((nrows, half), BF),
            vmem((slots, nrows), BF),
            vmem((half, dim), BF),
            vmem((half, hid), F32),
            vmem((half, dim), BF),
            vmem((nrows, dim), BF),
            vmem((nrows, hid // 2), BF),
            vmem((slots, hid // 2), BF),
            vmem((nrows, dim), BF),
            vmem((layers, nrows, dim), BF),
            vmem((nrows, hid), BF),
            dma((3,)),
            dma((6 * layers,)),
            dma((6 * layers, feats // 2)),
            dma((6 * layers, feats // 2)),
            dma((6 * layers, feats // 2)),
            dma((6 * layers, feats // 2)),
            dma((feats,)),
            dma((feats,)),
            dma((layers, patches)),
            dma((layers, patches)),
            dma((layers, patches)),
            dma((layers, patches)),
            dma((layers,)),
            dma((layers,)),
            dma((blocks,)),
            dma((blocks,)),
            dma((blocks,)),
        ],
        compiler_params=pltpu.CompilerParams(
            collective_id=0, has_side_effects=True, vmem_limit_bytes=62 * 2**20
        ),
    )
    return call(
        nodes,
        edges,
        send_rows.reshape(patches, cap),
        edge_slot.reshape(erows // LANES, LANES),
        receivers.reshape(erows // LANES, LANES),
        ein, eb, eo, egain, nin, nb, no, ngain,
    )


def solution(mesh):
    in_specs = (
        P("patch", None),
        P("patch", None),
        P("patch", None, None),
        P("patch"),
        P("patch"),
        P(None, None, None, "feat"),
        P(None, "feat"),
        P(None, "feat", None),
        P(),
        P(None, None, None, "feat"),
        P(None, "feat"),
        P(None, "feat", None),
        P(),
    )
    out_specs = (P("patch", None), P("patch", None))
    inner = functools.partial(body, mesh.shape["patch"], mesh.shape["feat"])
    return jax.shard_map(inner, mesh=mesh, in_specs=in_specs, out_specs=out_specs, check_vma=False)
```

time: 496 us -> 100 us (0.20)
  waiting for transfers between devices: 263 us -> 0 us
  Pallas kernels: 0 us -> 92.8 us
  local copies, waits for them, and re-layouts: 90.9 us -> 6.34 us
  matrix products: 62.5 us -> 0 us
  blocking collectives: 31.5 us -> 0 us
  starting transfers between devices: 19.7 us -> 0 us
  between operations: 14.5 us -> 0.64 us
  other arithmetic: 10.8 us -> 0 us
    all_gather x8 -> x0, waiting for transfers between devices: 186 us -> none  [the longest x3 86.8 us: body(): every_proj = lax.all_gather(sender_proj, 'patch', axis=0, tiled=True)]
    pallas_call x0 -> x1, Pallas kernels: none -> 92.8 us  [body(): call(nodes, edges, send_rows.reshape(patches, cap), edge_slot.reshape(ero...]
    gather x7 -> x0, local copies, waits for them, and re-layouts: 75.7 us -> none  [the longest x3 47.1 us: body(): fetched = every_proj[senders]]
    dot_general x42 -> x0, matrix products: 62.5 us -> none  [the longest x24 30.6 us: local_split_sum(): jnp.dot(hidden[:, first:first + share_width], weight[first:first + share_...]
    reduce_scatter x3 -> x0, waiting for transfers between devices: 62.1 us -> none  [body(): lax.psum_scatter(jnp.dot(incidence, update, preferred_element_type=jnp.fl...]
    all_gather x5 -> x0, blocking collectives: 31.5 us -> none  [the longest x3 21.3 us: body(): node_state = lax.all_gather(own_next, 'feat', axis=0, tiled=True)]
    all_to_all x4 -> x0, starting transfers between devices: 19.1 us -> none  [the longest x3 12.9 us: body(): lax.all_to_all(fetched, 'feat', split_axis=0, concat_axis=1, tiled=True)]
    all_to_all x4 -> x0, waiting for transfers between devices: 12.4 us -> none  [the longest x3 12.4 us: body(): lax.all_to_all(fetched, 'feat', split_axis=0, concat_axis=1, tiled=True)]
  transfers between devices with their start and end apart: 15 -> 0, of which waited for: 13 -> 0; matrix products, arithmetic and copies ran while one was open for 17% -> 0% of each run, Pallas kernels for 0% -> 0%
where the time goes in v1:
time: 100 us; the launch traced here: 99.8 us
  Pallas kernels  92.8 us (93%)
  local copies, waits for them, and re-layouts  6.34 us (6%)
    pallas_call x1, Pallas kernels, body(): call(nodes, edges, send_rows.reshape(patches, cap), edge_slot.reshape(ero...  92.8 us
    unnamed x2, local copies, waits for them, and re-layouts  6.34 us

profile of v1, /device:TPU:10, one launch (start us, length us, event | category | flops | bytes accessed | tf_op | source)
XLA Modules:
  0.0 99.8 jit_solution(280513594472657973)
XLA Ops:
  0.6 92.8 %shard_map.140 = (bf16[512,512]{1,0:T(8,128)(2,1)}, bf16[4096,512]{1,0:T(8,128)(2,1)}) custom-call(bf16[512,512]{1,0:T(8,128)(2,1)} %nodes_in.1, bf16[4096,512]{1,0:T(8,128)(2,1)} %edges_in.1, s32[8,128]{1,0:T(8,128)} %bitcast.5, s32[32,128]{1,0:T(8,128)} %bitcast.3, s32[32,128]{1,0:T(8,128)} %bitcast.4, bf16[3,3,512,128]{3,2,1,0:T(8,128)(2,1)} %ein.1, ...), custom_call_target="tpu_custom_call" | custom-call | tf_op jit(solution)/shard_map/pallas_call | solution.py:458
  93.5 1.9 %copy.17 = bf16[512,512]{1,0:T(8,128)(2,1)} copy(bf16[512,512]{1,0:T(8,128)(2,1)} %get-tuple-element.4) | data formatting | bytes 1048576
  95.4 4.5 %copy.18 = bf16[4096,512]{1,0:T(8,128)(2,1)} copy(bf16[4096,512]{1,0:T(8,128)(2,1)} %get-tuple-element.5) | data formatting | bytes 8388608

commit v2 on v1

--- a/solution.py
+++ b/solution.py
@@ -318,18 +318,31 @@
         if l + 1 < layers:
             start_weights(l + 1)
 
-        def work(b, carry, l=l):
+        def first(b, l=l):
             rows = pl.ds(pl.multiple_of(b * BLOCK, BLOCK), BLOCK)
-            hidden = silu(pre[rows, :] + dot(hot_slot[rows, :], table[l])).astype(BF)
-            message = norm(dot(hidden, w_eo[l]), egain[l : l + 1, :])
+            upd[rows, :] = silu(pre[rows, :] + dot(hot_slot[rows, :], table[l])).astype(BF)
+
+        def second(b, l=l):
+            rows = pl.ds(pl.multiple_of(b * BLOCK, BLOCK), BLOCK)
+            message = norm(dot(upd[rows, :], w_eo[l]), egain[l : l + 1, :])
             upd[rows, :] = message.astype(BF)
             edge[rows, :] = (edge[rows, :].astype(F32) + message).astype(BF)
+
+        def hand_out(b, l=l):
             if l == layers - 1:
                 out_local(b).start()
                 out_remote(b, core).start()
-            return carry
-
-        lax.fori_loop(0, blocks, work, 0)
+
+        def work(b, carry):
+            second(b - 1)
+            first(b)
+            hand_out(b - 1)
+            return carry
+
+        first(0)
+        lax.fori_loop(1, blocks, work, 0)
+        second(blocks - 1)
+        hand_out(blocks - 1)
         for b in range(nrows // BLOCK):
             rows = slice(b * BLOCK, (b + 1) * BLOCK)
             part[rows] = dot(hot_recv_t[rows, :], upd[...]).astype(BF)

time: 100 us -> 94.7 us (0.947)
  Pallas kernels: 92.8 us -> 87.5 us
    pallas_call x1, Pallas kernels: 92.8 us -> 87.5 us  [body(): call(nodes, edges, send_rows.reshape(patches, cap), edge_slot.reshape(ero...]
where the time goes in v2:
time: 94.7 us; the launch traced here: 94.5 us
  Pallas kernels  87.5 us (92%)
  local copies, waits for them, and re-layouts  6.34 us (7%)
    pallas_call x1, Pallas kernels, body(): call(nodes, edges, send_rows.reshape(patches, cap), edge_slot.reshape(ero...  87.5 us
    unnamed x2, local copies, waits for them, and re-layouts  6.34 us

profile of v2, /device:TPU:10, one launch (start us, length us, event | category | flops | bytes accessed | tf_op | source)
XLA Modules:
  0.0 94.5 jit_solution(8605185228388900805)
XLA Ops:
  0.6 87.5 %shard_map.140 = (bf16[512,512]{1,0:T(8,128)(2,1)}, bf16[4096,512]{1,0:T(8,128)(2,1)}) custom-call(bf16[512,512]{1,0:T(8,128)(2,1)} %nodes_in.1, bf16[4096,512]{1,0:T(8,128)(2,1)} %edges_in.1, s32[8,128]{1,0:T(8,128)} %bitcast.5, s32[32,128]{1,0:T(8,128)} %bitcast.3, s32[32,128]{1,0:T(8,128)} %bitcast.4, bf16[3,3,512,128]{3,2,1,0:T(8,128)(2,1)} %ein.1, ...), custom_call_target="tpu_custom_call" | custom-call | tf_op jit(solution)/shard_map/pallas_call | solution.py:471
  88.1 1.9 %copy.17 = bf16[512,512]{1,0:T(8,128)(2,1)} copy(bf16[512,512]{1,0:T(8,128)(2,1)} %get-tuple-element.4) | data formatting | bytes 1048576
  90.0 4.5 %copy.18 = bf16[4096,512]{1,0:T(8,128)(2,1)} copy(bf16[4096,512]{1,0:T(8,128)(2,1)} %get-tuple-element.5) | data formatting | bytes 8388608

commit v3 on v2

--- a/solution.py
+++ b/solution.py
@@ -278,7 +278,7 @@
         ] = dot(hot_send[mine, :], proj[...]).astype(BF)
         table_pass(l, me, core).start()
         if l == 0:
-            lax.fori_loop(0, lines, build_edge, 0)
+            lax.fori_loop(0, lines, build_edge, 0, unroll=2)
             load_edges.wait()
             for j in range(1, feats):
                 bias_copy(j, lax.rem(f + feats - j, feats)).wait_recv()
@@ -298,7 +298,7 @@
             )
             return carry
 
-        lax.fori_loop(0, blocks, begin, 0)
+        lax.fori_loop(0, blocks, begin, 0, unroll=2)
 
         def relay(j, carry, l=l):
             s = lax.rem(me + j, patches)
@@ -352,16 +352,14 @@
         advance(k0 + 5)
         acquire(k0 + 4)
         acquire(k0 + 5)
+        npre = pre.at[0:nrows]
+        npre[...] = dot(node[...], w_nin[l, 0])
         swap.wait()
         nb_row = bias(layers + l)
-        for b in range(nrows // BLOCK):
-            rows = slice(b * BLOCK, (b + 1) * BLOCK)
-            incoming = (part[rows].astype(F32) + other[l, rows].astype(F32)).astype(BF)
-            hidden = silu(
-                dot(node[rows], w_nin[l, 0]) + dot(incoming, w_nin[l, 1]) + nb_row
-            ).astype(BF)
-            change = norm(dot(hidden, w_no[l]), ngain[l : l + 1, :])
-            node[rows] = (node[rows].astype(F32) + change).astype(BF)
+        incoming = (part[...].astype(F32) + other[l].astype(F32)).astype(BF)
+        hidden = silu(npre[...] + dot(incoming, w_nin[l, 1]) + nb_row).astype(BF)
+        change = norm(dot(hidden, w_no[l]), ngain[l : l + 1, :])
+        node[...] = (node[...].astype(F32) + change).astype(BF)
 
         def drain(j, carry, l=l):
             table_copy(l, me, lax.rem(me + j, patches)).wait_send()

time: 94.7 us -> 94.6 us (level)
  no operation moved by 1% of the time
where the time goes in v3:
time: 94.6 us; the launch traced here: 94.3 us
  Pallas kernels  87.4 us (92%)
  local copies, waits for them, and re-layouts  6.34 us (7%)
    pallas_call x1, Pallas kernels, body(): call(nodes, edges, send_rows.reshape(patches, cap), edge_slot.reshape(ero...  87.4 us
    unnamed x2, local copies, waits for them, and re-layouts  6.34 us

profile of v3, /device:TPU:10, one launch (start us, length us, event | category | flops | bytes accessed | tf_op | source)
XLA Modules:
  0.0 94.3 jit_solution(5414854245451084498)
XLA Ops:
  0.6 87.4 %shard_map.140 = (bf16[512,512]{1,0:T(8,128)(2,1)}, bf16[4096,512]{1,0:T(8,128)(2,1)}) custom-call(bf16[512,512]{1,0:T(8,128)(2,1)} %nodes_in.1, bf16[4096,512]{1,0:T(8,128)(2,1)} %edges_in.1, s32[8,128]{1,0:T(8,128)} %bitcast.5, s32[32,128]{1,0:T(8,128)} %bitcast.3, s32[32,128]{1,0:T(8,128)} %bitcast.4, bf16[3,3,512,128]{3,2,1,0:T(8,128)(2,1)} %ein.1, ...), custom_call_target="tpu_custom_call" | custom-call | tf_op jit(solution)/shard_map/pallas_call | solution.py:469
  88.0 1.9 %copy.17 = bf16[512,512]{1,0:T(8,128)(2,1)} copy(bf16[512,512]{1,0:T(8,128)(2,1)} %get-tuple-element.4) | data formatting | bytes 1048576
  89.9 4.5 %copy.18 = bf16[4096,512]{1,0:T(8,128)(2,1)} copy(bf16[4096,512]{1,0:T(8,128)(2,1)} %get-tuple-element.5) | data formatting | bytes 8388608
